TPU v7x, 256 devices: a whole 4x4x8 slice. The times are simulated.
256 devices in a mesh: row: 32 (over z_lo, y, x), col: 8 (over z_hi, core).
Axes of the slice: x: 4, y: 4, z: 8 (z_hi: 4, z_lo: 2; z = z_hi * 2 + z_lo), core: 2. Of those that a mesh axis runs over, the one named last changes fastest.
Arguments:
- features: bfloat16 [512, 512, 1024], P('row', None, 'col'), may hold values from -6 to 6
- projection: bfloat16 [512, 4], replicated, may hold values from -0.25 to 0.25
- norm_gain: bfloat16 [2048], replicated, may hold values from 0.25 to 1.75
- norm_shift: bfloat16 [2048], replicated, may hold values from -6 to 6
- weight_in: bfloat16 [2048, 4096], P(None, 'col'), may hold values from -0.125 to 0.125
- weight_out: bfloat16 [4096, 1, 1024], P('col'), may hold values from -0.09375 to 0.09375
- cotangent: bfloat16 [512, 1, 1024], P('row', None, 'col'), may hold values from -6 to 6
Outputs:
- mixed: bfloat16 [512, 1, 1024], P('row', None, 'col')
- grad_features: bfloat16 [512, 512, 1024], P('row', None, 'col')
- grad_gain: float32 [2048], replicated
- grad_shift: float32 [2048], replicated
- grad_weight_in: bfloat16 [2048, 4096], P(None, 'col')
- grad_weight_out: bfloat16 [4096, 1, 1024], P('col')
All inputs are finite; a program needn't handle non-finite values.
Results may differ from a plain program's by a relative error of at most 0.013.
Values may be sent and summed in bfloat16 or wider, within the bound.
A program may use at most 64 MiB of HBM per device.

v0:
```python
import jax
import jax.numpy as jnp
from jax import lax
from jax.sharding import PartitionSpec as P


def layer_norm(inter, norm_gain, norm_shift):
    mean = jnp.mean(inter, axis=1, keepdims=True)
    centered = inter - mean
    rstd = lax.rsqrt(jnp.mean(centered * centered, axis=1, keepdims=True) + 1e-05)
    unit = centered * rstd
    normed = (unit * norm_gain.astype(jnp.float32) + norm_shift.astype(jnp.float32)).astype(
        jnp.bfloat16
    )
    return (normed, unit, rstd)


def on_device(features, projection, norm_gain, norm_shift, weight_in, weight_out, cotangent):
    batch = features.shape[0]
    embeds = features.shape[1]
    reduced = jnp.einsum(
        "bnd,nk->bdk", features, projection, preferred_element_type=jnp.float32
    ).astype(jnp.bfloat16)
    partial_inter = jnp.einsum(
        "bnd,bdk->bnk", features, reduced, preferred_element_type=jnp.float32
    ).reshape(batch, -1)
    inter = lax.psum(partial_inter, "col")
    normed, unit, rstd = layer_norm(inter, norm_gain, norm_shift)
    pre = jnp.dot(normed, weight_in, preferred_element_type=jnp.float32)
    act = jax.nn.silu(pre).astype(jnp.bfloat16)
    out_terms = jnp.einsum("bh,hfd->bfd", act, weight_out, preferred_element_type=jnp.float32)
    mixed = lax.psum_scatter(out_terms, "col", scatter_dimension=2, tiled=True).astype(jnp.bfloat16)
    full_grads = lax.all_gather(cotangent, "col", axis=2, tiled=True)
    dact = jnp.einsum("bfd,hfd->bh", full_grads, weight_out, preferred_element_type=jnp.float32)
    sigma = jax.nn.sigmoid(pre)
    dpre = (dact * sigma * (1.0 + pre * (1.0 - sigma))).astype(jnp.bfloat16)
    partial_dnormed = jnp.einsum("bh,ih->bi", dpre, weight_in, preferred_element_type=jnp.float32)
    dnormed = lax.psum(partial_dnormed, "col")
    gain_terms = jnp.sum(dnormed * unit, axis=0)
    shift_terms = jnp.sum(dnormed, axis=0)
    in_terms = jnp.einsum("bi,bh->ih", normed, dpre, preferred_element_type=jnp.float32)
    out_grad_terms = jnp.einsum("bh,bfd->hfd", act, full_grads, preferred_element_type=jnp.float32)
    grad_in, grad_out, grad_gain, grad_shift = lax.psum(
        (in_terms, out_grad_terms, gain_terms, shift_terms), "row"
    )
    scaled = dnormed * norm_gain.astype(jnp.float32)
    dinter = rstd * (
        scaled
        - jnp.mean(scaled, axis=1, keepdims=True)
        - unit * jnp.mean(scaled * unit, axis=1, keepdims=True)
    )
    dinter = dinter.reshape(batch, embeds, -1)
    dreduced = jnp.einsum("bnd,bnk->bdk", features, dinter, preferred_element_type=jnp.float32)
    grad_features = jnp.einsum("bnk,bdk->bnd", dinter, reduced, preferred_element_type=jnp.float32)
    grad_features = grad_features + jnp.einsum(
        "nk,bdk->bnd", projection, dreduced, preferred_element_type=jnp.float32
    )
    return (
        mixed,
        grad_features.astype(jnp.bfloat16),
        grad_gain,
        grad_shift,
        grad_in.astype(jnp.bfloat16),
        grad_out.astype(jnp.bfloat16),
    )


def solution(mesh):
    placed = (
        P("row", None, "col"),
        P(),
        P(),
        P(),
        P(None, "col"),
        P("col", None, None),
        P("row", None, "col"),
    )
    return jax.shard_map(
        on_device,
        mesh=mesh,
        in_specs=placed,
        out_specs=(
            P("row", None, "col"),
            P("row", None, "col"),
            P(),
            P(),
            P(None, "col"),
            P("col", None, None),
        ),
        check_vma=False,
    )
```

profile of v0, /device:TPU:32, one launch (start us, length us, event | category | flops | bytes accessed | tf_op | source)
XLA Modules:
  0.0 379.2 jit_solution(18031466390064069782)
XLA Ops:
  7.2 1.5 copy-done
  8.8 1.1 convolution_convert_fusion
  9.8 0.6 convolution_bitcast_fusion.1
  10.5 0.4 copy.15
  10.9 1.0 copy.16
  12.0 17.3 %all_gather.3 = bf16[16,1,1024]{2,0,1:T(8,128)(2,1)S(1)} all-gather(bf16[16,1,128]{2,0,1:T(8,128)(2,1)S(1)} %copy-done.7), channel_id=1, replica_groups=mesh['row'=32,'col'=8] {'col'}, dimensions={2}, use_global_device_ids=true | all-gather | bytes 36864 | tf_op jit(solution)/shard_map/all_gather | solution.py:33
  29.3 56.6 %all-reduce.5.cloned.1.call-done = f32[16,2048]{1,0:T(8,128)} async-done(((f32[16,2048]{1,0:T(8,128)}), f32[16,2048]{1,0:T(8,128)}) %all-reduce.5.cloned.1.call-update) | async-done | bytes 131088 | tf_op jit(solution)/shard_map/psum | solution.py:27
  85.8 1.0 reduce_sum.54
  86.9 1.1 multiply_reduce_fusion.2
  88.0 2.2 fusion.10
  90.2 1.9 convolution_bitcast_fusion
  92.0 0.4 fusion.2
  92.4 1.3 fusion.11
  93.8 2.7 fusion.9
  96.6 0.9 convolution_bitcast_fusion.2
  97.5 66.6 %all-reduce.7.cloned.1.call-done = f32[16,2048]{1,0:T(8,128)} async-done(((f32[16,2048]{1,0:T(8,128)}), f32[16,2048]{1,0:T(8,128)}) %all-reduce.7.cloned.1.call-update) | async-done | bytes 131088 | tf_op jit(solution)/shard_map/psum | solution.py:38
  164.1 1.1 multiply_reduce_fusion
  165.2 1.0 subtract_multiply_fusion
  166.2 0.3 copy.17
  166.5 0.3 copy.18
  166.9 2.8 fusion.12
  169.6 4.5 %fusion = bf16[16,512,128]{2,1,0:T(8,128)(2,1)} fusion(f32[16,512,128]{2,1,0:T(8,128)} %fusion.12, bf16[16,512,4]{1,2,0:T(4,128)(2,1)S(1)} %copy.18, bf16[16,512,128]{2,1,0:T(8,128)(2,1)S(1)} %copy-done, bf16[512,4]{0,1:T(4,128)(2,1)S(1)} %copy-done.4), kind=kOutput, calls=%fused_computation.1 | convolution fusion | flops 18874368 | bytes 8458240 | tf_op jit(solution)/shard_map/nk,bdk->bnd/dot_general | solution.py:55
  174.1 197.3 %all-reduce.8 = (f32[2048]{0:T(1024)}, f32[2048]{0:T(1024)}, bf16[2048,512]{1,0:T(8,128)(2,1)}, bf16[512,1,1024]{2,0,1:T(8,128)(2,1)}) all-reduce(f32[2048]{0:T(1024)S(1)} %get-tuple-element.6, f32[2048]{0:T(1024)S(1)} %get-tuple-element.9, f32[2048,512]{1,0:T(8,128)} %fusion.9, ...), channel_id=1, replica_groups=mesh['row'=32,'col'=8] {'row'}, use_global_device_ids=true, to_apply=%region_8.9 | all-reduce | flops 1576960 | bytes 9469952 | tf_op jit(solution)/shard_map/psum | solution.py:43
  371.3 1.3 convert_element_type.36
  (27 shorter events, 0.2 us)
Async XLA Ops:
  7.2 1.6 copy-start
  7.2 78.6 %all-reduce.5.cloned.1.call-start = ((), (), s32[]{:S(2)}) async-start(), calls=%async_computation.1 | async-start | bytes 262144 | tf_op jit(solution)/shard_map/psum | solution.py:27
  9.8 2.1 copy-start.5
  9.8 2.1 copy-start.6
  9.8 2.2 copy-start.7
  11.9 152.2 %all-reduce.7.cloned.1.call-start = ((), (), s32[]{:S(2)}) async-start(), calls=%async_computation.3 | async-start | bytes 262144 | tf_op jit(solution)/shard_map/psum | solution.py:38
  88.0 4.1 %copy-start.3 = (bf16[512,1,1024]{2,0,1:T(8,128)(2,1)S(1)}, bf16[512,1,1024]{2,0,1:T(8,128)(2,1)}, u32[]{:S(2)}) copy-start(bf16[512,1,1024]{2,0,1:T(8,128)(2,1)} %param.12) | copy-start | bytes 3145732
  90.2 2.3 copy-start.1
  92.0 1.8 copy-start.2
  93.8 277.6 %reduce-scatter.2.cloned.1.call-start = ((), (), s32[]{:S(2)}) async-start(), calls=%async_computation.2 | async-start | bytes 73728 | tf_op jit(solution)/shard_map/reduce_scatter | solution.py:32
  166.8 2.8 copy-start.4
Sparse Core Ops, SparseCore 0:
  12.0 73.7 all-reduce.4
  93.9 70.1 all-reduce.6
  166.6 35.4 reduce-scatter.1
where the time goes:
time: 380 us; the launch traced here: 379 us
  blocking collectives  215 us (57%)
  waiting for transfers between devices  123 us (32%)
  matrix products  18.3 us (5%)
  between operations  13.9 us (4%)
  other arithmetic  5.58 us (1%)
    psum x1, blocking collectives, on_device(): lax.psum((in_terms, out_grad_terms, gain_terms, shift_terms), 'row')  197 us
    psum x1, waiting for transfers between devices, on_device(): dnormed = lax.psum(partial_dnormed, 'col')  66.6 us
    psum x1, waiting for transfers between devices, on_device(): inter = lax.psum(partial_inter, 'col')  56.6 us
    all_gather x1, blocking collectives, on_device(): full_grads = lax.all_gather(cotangent, 'col', axis=2, tiled=True)  17.3 us
  transfers between devices with their start and end apart: 3, of which 2 were waited for; matrix products, arithmetic and copies ran while one was open for 4% of the time, Pallas kernels for 0%

commit v1 on v0

--- a/solution.py
+++ b/solution.py
@@ -24,7 +24,7 @@
     partial_inter = jnp.einsum(
         "bnd,bdk->bnk", features, reduced, preferred_element_type=jnp.float32
     ).reshape(batch, -1)
-    inter = lax.psum(partial_inter, "col")
+    inter = jnp.sum(lax.all_gather(partial_inter, "col"), axis=0)
     normed, unit, rstd = layer_norm(inter, norm_gain, norm_shift)
     pre = jnp.dot(normed, weight_in, preferred_element_type=jnp.float32)
     act = jax.nn.silu(pre).astype(jnp.bfloat16)

time: 380 us -> 340 us (0.89)
  waiting for transfers between devices: 123 us -> 84.3 us
    psum x1 -> x0, waiting for transfers between devices: 56.6 us -> none  [on_device(): inter = lax.psum(partial_inter, 'col')]
    all_gather x0 -> x1, waiting for transfers between devices: none -> 14.3 us  [on_device(): inter = jnp.sum(lax.all_gather(partial_inter, 'col'), axis=0)]
  transfers between devices with their start and end apart: 3 -> 3, of which waited for: 2 -> 2; matrix products, arithmetic and copies ran while one was open for 4% -> 3% of each run, Pallas kernels for 0% -> 0%
where the time goes in v1:
time: 340 us
  blocking collectives  215 us (63%)
  waiting for transfers between devices  84.3 us (25%)
  matrix products  18.2 us (5%)
  between operations  13.9 us (4%)
  other arithmetic  5.14 us (2%)
  local copies, waits for them, and re-layouts  3.53 us (1%)
    psum x1, blocking collectives, on_device(): lax.psum((in_terms, out_grad_terms, gain_terms, shift_terms), 'row')  198 us
    psum x1, waiting for transfers between devices, on_device(): dnormed = lax.psum(partial_dnormed, 'col')  69.9 us
    all_gather x1, blocking collectives, on_device(): full_grads = lax.all_gather(cotangent, 'col', axis=2, tiled=True)  17.3 us
    all_gather x1, waiting for transfers between devices, on_device(): inter = jnp.sum(lax.all_gather(partial_inter, 'col'), axis=0)  14.3 us
  transfers between devices with their start and end apart: 3, of which 2 were waited for; matrix products, arithmetic and copies ran while one was open for 3% of the time, Pallas kernels for 0%

profile of v1, /device:TPU:32, one launch (start us, length us, event | category | flops | bytes accessed | tf_op | source)
XLA Modules:
  0.0 340.1 jit_solution(1303184620530049699)
XLA Ops:
  7.2 1.5 copy-done
  8.8 1.1 convolution_convert_fusion
  9.8 0.6 convolution_bitcast_fusion.1
  10.5 0.4 copy.19
  10.9 1.0 copy.20
  12.0 17.3 %all_gather.7 = bf16[16,1,1024]{2,0,1:T(8,128)(2,1)S(1)} all-gather(bf16[16,1,128]{2,0,1:T(8,128)(2,1)S(1)} %copy-done.6), channel_id=1, replica_groups=mesh['row'=32,'col'=8] {'col'}, dimensions={2}, use_global_device_ids=true | all-gather | bytes 36864 | tf_op jit(solution)/shard_map/all_gather | solution.py:33
  29.3 14.3 %all-gather.2.cloned.1.call-done = f32[8,16,2048]{2,1,0:T(8,128)} async-done(((f32[1,16,2048]{2,1,0:T(8,128)}), f32[8,16,2048]{2,1,0:T(8,128)}) %all-gather.2.cloned.1.call-update) | async-done | bytes 1048592 | tf_op jit(solution)/shard_map/all_gather | solution.py:27
  43.6 1.5 fusion.11
  45.1 0.2 multiply_reduce_fusion.2
  45.3 2.1 fusion.10
  47.4 1.9 convolution_bitcast_fusion
  49.3 0.4 fusion.2
  49.6 1.3 fusion.12
  51.0 2.7 fusion.9
  53.8 0.9 convolution_bitcast_fusion.2
  54.7 69.9 %all-reduce.4.cloned.1.call-done = f32[16,2048]{1,0:T(8,128)} async-done(((f32[16,2048]{1,0:T(8,128)}), f32[16,2048]{1,0:T(8,128)}) %all-reduce.4.cloned.1.call-update) | async-done | bytes 131088 | tf_op jit(solution)/shard_map/psum | solution.py:38
  124.6 1.1 multiply_reduce_fusion
  125.8 1.0 subtract_multiply_fusion
  126.8 0.3 copy.23
  127.0 0.3 copy.24
  127.4 2.8 fusion.13
  130.1 4.5 %fusion = bf16[16,512,128]{2,1,0:T(8,128)(2,1)} fusion(f32[16,512,128]{2,1,0:T(8,128)} %fusion.13, bf16[16,512,4]{1,2,0:T(4,128)(2,1)S(1)} %copy.24, bf16[16,512,128]{2,1,0:T(8,128)(2,1)S(1)} %copy-done, bf16[512,4]{0,1:T(4,128)(2,1)S(1)} %copy-done.3), kind=kOutput, calls=%fused_computation.1 | convolution fusion | flops 18874368 | bytes 8458240 | tf_op jit(solution)/shard_map/nk,bdk->bnd/dot_general | solution.py:55
  134.6 197.7 %all-reduce.5 = (f32[2048]{0:T(1024)}, f32[2048]{0:T(1024)}, bf16[2048,512]{1,0:T(8,128)(2,1)}, bf16[512,1,1024]{2,0,1:T(8,128)(2,1)}) all-reduce(f32[2048]{0:T(1024)S(1)} %get-tuple-element.8, f32[2048]{0:T(1024)S(1)} %get-tuple-element.11, f32[2048,512]{1,0:T(8,128)} %fusion.9, ...), channel_id=1, replica_groups=mesh['row'=32,'col'=8] {'row'}, use_global_device_ids=true, to_apply=%region_8.9 | all-reduce | flops 1576960 | bytes 9469952 | tf_op jit(solution)/shard_map/psum | solution.py:43
  332.3 1.3 convert_element_type.36
  (25 shorter events, 0.2 us)
Async XLA Ops:
  7.2 1.6 copy-start
  7.2 36.4 %all-gather.2.cloned.1.call-start = ((), (), s32[]{:S(2)}) async-start(), calls=%async_computation.1 | async-start | bytes 1179648 | tf_op jit(solution)/shard_map/all_gather | solution.py:27
  9.8 2.1 copy-start.4
  9.8 2.1 copy-start.5
  9.8 2.2 copy-start.6
  11.9 112.7 %all-reduce.4.cloned.1.call-start = ((), (), s32[]{:S(2)}) async-start(), calls=%async_computation.3 | async-start | bytes 262144 | tf_op jit(solution)/shard_map/psum | solution.py:38
  45.3 4.0 %copy-start.2 = (bf16[512,1,1024]{2,0,1:T(8,128)(2,1)S(1)}, bf16[512,1,1024]{2,0,1:T(8,128)(2,1)}, u32[]{:S(2)}) copy-start(bf16[512,1,1024]{2,0,1:T(8,128)(2,1)} %param.12) | copy-start | bytes 3145732
  47.4 2.3 copy-start.1
  53.7 278.5 %reduce-scatter.2.cloned.1.call-start = ((), (), s32[]{:S(2)}) async-start(), calls=%async_computation.2 | async-start | bytes 73728 | tf_op jit(solution)/shard_map/reduce_scatter | solution.py:32
  127.4 2.8 copy-start.3
Sparse Core Ops, SparseCore 0:
  12.0 31.5 all-gather.1
  53.9 70.7 all-reduce.3
  127.3 35.4 reduce-scatter.1
